TPU v7x, 128 devices: a whole 4x4x4 slice. The times are simulated.
128 devices in a mesh: dp: 32 (over y, z, core), tensor: 4 (over x).
Axes of the slice: x: 4, y: 4, z: 4, core: 2. Of those that a mesh axis runs over, the one named last changes fastest.
Arguments:
- grads: float32 [32, 1024, 8192], P('dp', 'tensor'), may hold values from -6 to 6
- errors: float32 [32, 1024, 8192], P('dp', 'tensor'), may hold values from -6 to 6
- q_start: float32 [8192, 64], replicated, may hold values from -6 to 6
Outputs:
- new_errors: float32 [32, 1024, 8192], P('dp', 'tensor')
- p_orth: float32 [1024, 64], P('tensor')
- q_new: float32 [8192, 64], replicated
All inputs are finite; a program needn't handle non-finite values.
Results may differ from a plain program's by a relative error of at most 0.0001.
Values sent between devices are 32-bit elements; how exact they have to be, the bound alone decides.
A program may use at most 128 MiB of HBM per device.

v0:
```python
import jax
import jax.numpy as jnp
from jax import lax
from jax.sharding import PartitionSpec as P


def local(grads, errors, q_start):
    high = lax.Precision.HIGHEST
    merged = grads[0] + errors[0]
    replicas = lax.axis_size("dp")
    local_left = jnp.dot(merged, q_start, precision=high) / replicas
    sketch = lax.psum(local_left, "dp")
    gram = lax.psum(jnp.dot(sketch.T, sketch, precision=high), "tensor")
    gram = gram + 1e-05 * (jnp.trace(gram) / gram.shape[0]) * jnp.eye(
        gram.shape[0], dtype=jnp.float32
    )
    lower = jnp.linalg.cholesky(gram)
    p_orth = lax.linalg.triangular_solve(
        lower, sketch, left_side=False, lower=True, transpose_a=True
    )
    q_new = lax.psum(jnp.dot(merged.T, p_orth, precision=high) / replicas, ("dp", "tensor"))
    approx = jnp.dot(p_orth, q_new.T, precision=high)
    new_errors = merged - approx
    return (new_errors[None], p_orth, q_new)


def solution(mesh):
    return jax.shard_map(
        local,
        mesh=mesh,
        in_specs=(P("dp", "tensor", None), P("dp", "tensor", None), P()),
        out_specs=(P("dp", "tensor", None), P("tensor", None), P()),
        check_vma=False,
    )
```

profile of v0, /device:TPU:1, one launch (start us, length us, event | category | flops | bytes accessed | tf_op | source)
XLA Modules:
  0.0 334.6 jit_solution(5655403023204069934)
XLA Ops:
  7.2 0.0 copy-start
  7.2 0.0 all-reduce.3.cloned.1.call-start
  7.2 1.5 copy-done
  8.8 12.0 %fusion.4 = f32[256,64]{0,1:T(8,128)} fusion(f32[8192,64]{0,1:T(8,128)S(1)} %copy-done, f32[1,256,8192]{2,1,0:T(8,128)} %param.3, f32[1,256,8192]{2,1,0:T(8,128)} %param.4), kind=kOutput, calls=%fused_computation.6 | convolution fusion | flops 1612726272 | bytes 18939904 | tf_op jit(solution)/shard_map/dot_general | solution.py:11
  20.7 0.0 all-reduce.3.cloned.1.call-update
  20.7 0.0 all-reduce.5.cloned.1.call-start
  20.8 99.0 %all-reduce.3.cloned.1.call-done = f32[256,64]{0,1:T(8,128)} async-done(((f32[256,64]{0,1:T(8,128)}), f32[256,64]{0,1:T(8,128)}) %all-reduce.3.cloned.1.call-update) | async-done | bytes 65552 | tf_op jit(solution)/shard_map/psum | solution.py:12
  119.7 1.1 fusion.13
  120.9 13.3 %psum.22 = f32[64,64]{1,0:T(8,128)S(1)} all-reduce(f32[64,64]{1,0:T(8,128)S(1)} %fusion.13), channel_id=1, replica_groups=mesh['dp'=32,'tensor'=4] {'tensor'}, use_global_device_ids=true, to_apply=%region_1.0 | all-reduce | flops 4096 | bytes 32768 | tf_op jit(solution)/shard_map/psum | solution.py:13
  134.2 0.6 select_reduce_fusion.1
  135.4 0.1 copy.6
  135.5 5.8 %cholesky.17 = f32[64,64]{1,0:T(8,128)S(1)} custom-call(f32[64,64]{1,0:T(8,128)S(1)} %fusion.10), custom_call_target="Cholesky" | custom-call | tf_op jit(solution)/shard_map/jit(cholesky)/cholesky | solution.py:17
  141.4 0.6 compare_reduce_fusion
  142.1 0.7 fusion.7
  142.7 4.9 %custom-call.6 = f32[1,64,64]{1,2,0:T(8,128)S(1)} custom-call(f32[1,64,64]{2,1,0:T(8,128)S(1)} %fusion.7), custom_call_target="InvertDiagBlocksLowerTriangular" | custom-call | tf_op jit(solution)/shard_map/triangular_solve | solution.py:18
  147.6 1.1 fusion.8
  148.7 0.0 copy-start.2
  148.7 12.8 %convolution_multiply_fusion = f32[8192,64]{0,1:T(8,128)} fusion(f32[256,64]{0,1:T(8,128)S(1)} %fusion.8, f32[1,256,8192]{2,1,0:T(8,128)} %param.3, f32[1,256,8192]{2,1,0:T(8,128)} %param.4), kind=kOutput, calls=%fused_computation.2 | convolution fusion | flops 1613234176 | bytes 18939904 | tf_op jit(solution)/shard_map/dot_general | solution.py:21
  161.5 0.0 all-reduce.5.cloned.1.call-update
  161.6 151.1 %all-reduce.5.cloned.1.call-done = f32[8192,64]{0,1:T(8,128)} async-done(((f32[8192,64]{0,1:T(8,128)}), f32[8192,64]{0,1:T(8,128)}) %all-reduce.5.cloned.1.call-update) | async-done | bytes 2097168 | tf_op jit(solution)/shard_map/psum | solution.py:21
  312.7 0.0 copy-done.2
  312.7 13.8 %fusion = f32[1,256,8192]{2,1,0:T(8,128)} fusion(f32[256,64]{0,1:T(8,128)S(1)} %fusion.8, f32[8192,64]{0,1:T(8,128)} %all-reduce.5.cloned.1.call-done, f32[1,256,8192]{2,1,0:T(8,128)} %param.3, f32[1,256,8192]{2,1,0:T(8,128)} %param.4), kind=kOutput, calls=%fused_computation.1 | convolution fusion | flops 1614807040 | bytes 27328512 | tf_op jit(solution)/shard_map/dot_general | solution.py:22
  326.4 0.0 copy-done.1
  326.4 1.3 copy.9
  (4 shorter events, 0.1 us)
Async XLA Ops:
  7.2 1.6 copy-start
  7.2 112.6 %all-reduce.3.cloned.1.call-start = ((), (), s32[]{:S(2)}) async-start(), calls=%async_computation | async-start | bytes 131072 | tf_op jit(solution)/shard_map/psum | solution.py:12
  20.7 291.9 %all-reduce.5.cloned.1.call-start = ((), (), s32[]{:S(2)}) async-start(), calls=%async_computation.1 | async-start | bytes 4194304 | tf_op jit(solution)/shard_map/psum | solution.py:21
  148.7 164.0 %copy-start.2 = (f32[256,64]{0,1:T(8,128)}, f32[256,64]{0,1:T(8,128)S(1)}, u32[]{:S(2)}) copy-start(f32[256,64]{0,1:T(8,128)S(1)} %fusion.8) | copy-start | bytes 196612
  312.7 13.8 %copy-start.1 = (f32[8192,64]{0,1:T(8,128)S(1)}, f32[8192,64]{0,1:T(8,128)}, u32[]{:S(2)}) copy-start(f32[8192,64]{0,1:T(8,128)} %all-reduce.5.cloned.1.call-done) | copy-start | bytes 6291460
Sparse Core Ops, SparseCore 0:
  20.9 98.8 all-reduce.2
  161.7 150.9 all-reduce.4
where the time goes:
time: 335 us
  waiting for transfers between devices  250 us (75%)
  matrix products  40.7 us (12%)
  between operations  14.8 us (4%)
  blocking collectives  13.3 us (4%)
  other arithmetic  12.7 us (4%)
    psum x1, waiting for transfers between devices, local(): lax.psum(jnp.dot(merged.T, p_orth, precision=high) / replicas, ('dp', 'te...  151 us
    psum x1, waiting for transfers between devices, local(): sketch = lax.psum(local_left, 'dp')  99 us
    dot_general x1, matrix products, local(): approx = jnp.dot(p_orth, q_new.T, precision=high)  13.8 us
    psum x1, blocking collectives, local(): gram = lax.psum(jnp.dot(sketch.T, sketch, precision=high), 'tensor')  13.3 us
    dot_general x1, matrix products, local(): jnp.dot(merged.T, p_orth, precision=high) / replicas  12.8 us
    dot_general x1, matrix products, local(): local_left = jnp.dot(merged, q_start, precision=high) / replicas  12 us
  transfers between devices with their start and end apart: 2, of which 2 were waited for; matrix products, arithmetic and copies ran while one was open for 0% of the time, Pallas kernels for 0%

commit v1 on v0

v1 whole, which is shorter than its diff:
```python
import functools

import jax
import jax.numpy as jnp
from jax import lax
from jax.experimental import pallas as pl
from jax.experimental.pallas import tpu as pltpu
from jax.sharding import PartitionSpec as P

MESH = pl.DeviceIdType.MESH
F32, BF16 = jnp.float32, jnp.bfloat16
HIGH = lax.Precision.HIGHEST
ROWS, COLS, RANK, HALF = 256, 8192, 64, 32
BLK = 128
NBLK = ROWS // BLK
SLAB = COLS // 4
TILE = 128
GROUPS = ((0, 16), (16, 8), (24, 8))
AXIS_PEERS = [(1, 0, 0), (2, 0, 0), (3, 0, 0), (0, 1, 0), (0, 2, 0), (0, 3, 0), (0, 0, 1), (0, 0, 2), (0, 0, 3)]
ALL_PEERS = [(a, b, c) for a in range(4) for b in range(4) for c in range(4) if (a, b, c) != (0, 0, 0) and 0 in (a, b, c)]


def split(value):
    high = value.astype(BF16)
    return high, (value - high.astype(F32)).astype(BF16)


def device(x, y, z, c):
    return ((y * 4 + z) * 2 + c, x)


def dot_nt(a, b, precision=None):
    return lax.dot_general(a, b, (((1,), (1,)), ((), ())), precision=precision, preferred_element_type=F32)


def exchange(g_hbm, e_hbm, q_hbm, m_ref, z_ref, s_ref, w_ref,
             ebuf, qbuf, qs, hm, spart, sprx, srx, zbuf, zrx, rx1, ph2, rx2, zfin, gsl, lhs,
             in_sem, p_send, p_recv, s_send, s_recv, sp_send, sp_recv, g_send, g_recv,
             zp_send, zp_recv, r1_send, r1_recv, r2_send, r2_recv, a1_send, a1_recv, a2_send, a2_recv,
             f_send, f_recv):
    d = lax.axis_index("dp")
    x = lax.axis_index("tensor")
    y, z, c = d // 8, (d // 2) % 4, d % 2
    me = y * 4 + z
    partner = device(x, y, z, 1 - c)
    mine = pl.multiple_of(c * HALF, HALF)
    other = pl.multiple_of((1 - c) * HALF, HALF)

    def remote(src, dst, send, recv, target):
        return pltpu.make_async_remote_copy(src_ref=src, dst_ref=dst, send_sem=send, recv_sem=recv, device_id=target, device_id_type=MESH)

    loads = {}
    for b in range(NBLK):
        for k in range(4):
            rows, cols = pl.ds(b * BLK, BLK), pl.ds(k * SLAB, SLAB)
            parts = []
            if b == 0:
                parts.append(pltpu.make_async_copy(q_hbm.at[:, cols], qbuf.at[:, cols], in_sem.at[k, 2]))
            parts.append(pltpu.make_async_copy(g_hbm.at[rows, cols], m_ref.at[rows, cols], in_sem.at[b * 4 + k, 0]))
            parts.append(pltpu.make_async_copy(e_hbm.at[rows, cols], ebuf.at[rows, cols], in_sem.at[b * 4 + k, 1]))
            for part in parts:
                part.start()
            loads[b, k] = parts

    barrier = pltpu.get_barrier_semaphore()
    pl.semaphore_signal(barrier, inc=1, device_id=partner, device_id_type=MESH)
    for dx, dy, dz in ALL_PEERS:
        pl.semaphore_signal(barrier, inc=1, device_id=device((x + dx) % 4, (y + dy) % 4, (z + dz) % 4, c), device_id_type=MESH)

    def left_block(b, k):
        for part in loads[b, k]:
            part.wait()

        @pl.loop(0, SLAB // 256)
        def _(i):
            cols = pl.ds(pl.multiple_of(k * SLAB + i * 256, 256), 256)
            if b == 0:
                q_high, q_mid = split(qbuf[:, cols])
                qs[0:RANK, cols] = q_high
                qs[RANK:, cols] = q_mid
            rows = slice(b * BLK, (b + 1) * BLK)
            merged = m_ref[rows, cols] + ebuf[rows, cols]
            m_ref[rows, cols] = merged
            high, mid = split(merged)
            hm[b, 0:BLK, cols] = high
            hm[b, BLK:, cols] = mid

        cols = slice(k * SLAB, (k + 1) * SLAB)
        return dot_nt(qs[:, cols], hm[b, :, cols])

    def pair_copy(b):
        return remote(spart.at[b, pl.ds(other, HALF)], sprx.at[b], p_send.at[b], p_recv.at[b], partner)

    def left_send(b):
        copy = pair_copy(b)
        copy.wait()
        srx[b, me] = spart[b, pl.ds(mine, HALF)] + sprx[b]

        @pl.loop(1, 16)
        def _(r):
            target = device(x, (y + r // 4) % 4, (z + r % 4) % 4, c)
            remote(srx.at[b, me], srx.at[b, me], s_send.at[b], s_recv.at[b], target).start()

    for b in range(NBLK):
        total = jnp.zeros((2 * RANK, 2 * BLK), F32)
        for k in range(4):
            total = total + left_block(b, k)
            if b > 0 and k == 0:
                left_send(b - 1)
        total = total[:RANK] + total[RANK:]
        spart[b] = total[:, :BLK] + total[:, BLK:]
        if b == 0:
            pl.semaphore_wait(barrier, 1 + len(ALL_PEERS))
        pair_copy(b).start()
    left_send(NBLK - 1)

    def whole_copy(b):
        place = (pl.ds(mine, HALF), pl.ds(b * BLK, BLK))
        return remote(s_ref.at[place], s_ref.at[place], sp_send.at[b], sp_recv.at[b], partner)

    for b in range(NBLK):
        fifteen = srx.at[b, pl.ds(0, 15)]
        pltpu.make_async_copy(fifteen, fifteen, s_recv.at[b]).wait()
        pltpu.make_async_copy(fifteen, fifteen, s_send.at[b]).wait()
        total = srx[b, 0]
        for r in range(1, 16):
            total = total + srx[b, r]
        s_ref[pl.ds(mine, HALF), b * BLK:(b + 1) * BLK] = total * (1.0 / 32)
        whole_copy(b).start()
    for b in range(NBLK):
        whole_copy(b).wait()

    sketch = s_ref[...]
    high, mid = split(sketch)
    both = jnp.concatenate([high, mid], axis=0)
    for b in range(NBLK):
        part = both[:, b * BLK:(b + 1) * BLK]
        lhs[b] = jnp.concatenate([part, part], axis=1)

    gsl[x] = jnp.concatenate([dot_nt(sketch, sketch, HIGH), jnp.zeros((RANK, RANK), F32)], axis=1)
    for k in range(3):
        remote(gsl.at[x], gsl.at[x], g_send, g_recv, device((x + k + 1) % 4, y, z, c)).start()

    first = (jnp.where(c == 0, x, y), jnp.where(c == 0, y, x), z)

    def moved(g, da, db, dc):
        if g == 2:
            return device((x + db) % 4, (y + dc) % 4, (z + da) % 4, c)
        flip = c if g == 0 else 1 - c
        dx = jnp.where(flip == 0, da, dc)
        dy = jnp.where(flip == 0, db, da)
        dz = jnp.where(flip == 0, dc, db)
        return device((x + dx) % 4, (y + dy) % 4, (z + dz) % 4, c)

    xy0, xy1 = c == 0, c == 1
    second = (jnp.where(c == 0, y, z), jnp.where(c == 0, z, y), x)
    third = (jnp.where(c == 0, z, x), jnp.where(c == 0, x, z), y)

    def zpair(s, k):
        cols = pl.ds(pl.multiple_of(k * SLAB, SLAB), SLAB)
        return remote(zbuf.at[pl.ds(other, HALF), cols], zrx.at[s], zp_send.at[s], zp_recv.at[s], partner)

    def order(s):
        return lax.rem(x + y + z + s, 4)

    def slab_sum(s):
        k = order(s)
        zpair(s, k).wait()

        @pl.loop(0, SLAB // 512)
        def _(i):
            here = pl.ds(pl.multiple_of(i * 512, 512), 512)
            cols = pl.ds(pl.multiple_of(k * SLAB + i * 512, 512), 512)
            zbuf[pl.ds(mine, HALF), cols] += zrx[s, :, here]

        for g, (row, rows) in enumerate(GROUPS):
            step = lax.rem(k - first[g] + 4, 4)

            @pl.when(step != 0)
            def _():
                src = zbuf.at[pl.ds(pl.multiple_of(mine + row, 8), rows), pl.ds(pl.multiple_of(k * SLAB, SLAB), SLAB)]
                dst = rx1.at[step - 1, pl.ds(row, rows)]
                remote(src, dst, r1_send.at[g], r1_recv.at[g], moved(g, step, 0, 0)).start()

    for s in range(4):
        k = order(s)

        @pl.loop(0, SLAB // 256)
        def _(i):
            cols = pl.ds(pl.multiple_of(k * SLAB + i * 256, 256), 256)
            total = jnp.dot(lhs[0], hm[0, :, cols], preferred_element_type=F32)
            for b in range(1, NBLK):
                total = total + jnp.dot(lhs[b], hm[b, :, cols], preferred_element_type=F32)
            zbuf[:, cols] = total[:RANK] + total[RANK:]

        zpair(s, k).start()
        if s > 0:
            slab_sum(s - 1)
    slab_sum(3)

    for g, (row, rows) in enumerate(GROUPS):
        three = rx1.at[pl.ds(0, 3), pl.ds(row, rows)]
        pltpu.make_async_copy(three, three, r1_recv.at[g]).wait()
        cols = pl.ds(pl.multiple_of(first[g] * SLAB, SLAB), SLAB)
        ph2[row:row + rows] = (
            (zbuf[pl.ds(pl.multiple_of(mine + row, 8), rows), cols] + rx1[0, row:row + rows])
            + (rx1[1, row:row + rows] + rx1[2, row:row + rows])
        )

        @pl.loop(1, 16)
        def _(r):
            db, dc = r // 4, r % 4
            tile = lax.rem(second[g] + db, 4) * 4 + lax.rem(third[g] + dc, 4)
            src = ph2.at[pl.ds(row, rows), pl.ds(pl.multiple_of(tile * TILE, TILE), TILE)]
            remote(src, rx2.at[r - 1, pl.ds(row, rows)], r2_send.at[g], r2_recv.at[g], moved(g, 0, db, dc)).start()

    three = gsl.at[pl.ds(0, 3)]
    pltpu.make_async_copy(three, three, g_recv).wait()
    pltpu.make_async_copy(three, three, g_send).wait()
    gram = (gsl[0] + gsl[1]) + (gsl[2] + gsl[3])
    lane = lax.broadcasted_iota(jnp.int32, (RANK, 2 * RANK), 1)
    sub = lax.broadcasted_iota(jnp.int32, (RANK, 2 * RANK), 0)
    diagonal = jnp.where(lane == sub, gram, 0.0)
    trace = jnp.sum(jnp.sum(diagonal, axis=1, keepdims=True), axis=0, keepdims=True)
    mat = gram + jnp.where(lane == sub, 1e-05 * (trace / RANK), 0.0) + jnp.where(lane == sub + RANK, 1.0, 0.0)
    row_id = lax.broadcasted_iota(jnp.int32, (RANK, 1), 0)
    for j in range(RANK):
        pivot = mat[j:j + 1, :]
        factor = jnp.where(row_id > j, mat[:, j:j + 1] / mat[j:j + 1, j:j + 1], 0.0)
        mat = mat - factor * pivot
    scale = jnp.sum(jnp.where(lane == sub, mat, 0.0), axis=1, keepdims=True)
    w_ref[...] = mat[:, RANK:] / jnp.sqrt(scale)

    for g, (row, rows) in enumerate(GROUPS):
        fifteen = rx2.at[pl.ds(0, 15), pl.ds(row, rows)]
        pltpu.make_async_copy(fifteen, fifteen, r2_recv.at[g]).wait()
        tile = second[g] * 4 + third[g]
        total = ph2[row:row + rows, pl.ds(pl.multiple_of(tile * TILE, TILE), TILE)]
        for r in range(15):
            total = total + rx2[r, row:row + rows]
        place = (pl.ds(pl.multiple_of(mine + row, 8), rows), pl.ds(pl.multiple_of(first[g] * SLAB + tile * TILE, TILE), TILE))
        z_ref[place] = total

        @pl.loop(1, 16)
        def _(r):
            remote(z_ref.at[place], z_ref.at[place], a1_send.at[g], a1_recv.at[g], moved(g, 0, r // 4, r % 4)).start()

    def slab(g, v):
        row, rows = GROUPS[g]
        return z_ref.at[pl.ds(pl.multiple_of(mine + row, 8), rows), pl.ds(pl.multiple_of(v * SLAB, SLAB), SLAB)]

    def forward(g, step):
        here = slab(g, lax.rem(first[g] + step, 4))
        return remote(here, here, f_send.at[g, step], f_recv.at[g, step], partner)

    def along(g, step):
        here = slab(g, first[g])
        return remote(here, here, a2_send.at[g, step - 1], a2_recv.at[g, step - 1], moved(g, step, 0, 0))

    for g, (row, rows) in enumerate(GROUPS):
        fifteen = z_ref.at[pl.ds(pl.multiple_of(mine + row, 8), rows), pl.ds(0, 15 * TILE)]
        pltpu.make_async_copy(fifteen, fifteen, a1_recv.at[g]).wait()
        for step in (2, 1, 3):
            along(g, step).start()
        forward(g, 0).start()
    for step in (1, 3, 2):
        for g in range(3):
            along(g, step).wait_recv()
            forward(g, 4 - step).start()

    for g, (row, rows) in enumerate(GROUPS):
        three = rx1.at[pl.ds(0, 3), pl.ds(row, rows)]
        pltpu.make_async_copy(three, three, r1_send.at[g]).wait()
        fifteen = rx2.at[pl.ds(0, 15), pl.ds(row, rows)]
        pltpu.make_async_copy(fifteen, fifteen, r2_send.at[g]).wait()
        fifteen = z_ref.at[pl.ds(pl.multiple_of(mine + row, 8), rows), pl.ds(0, 15 * TILE)]
        pltpu.make_async_copy(fifteen, fifteen, a1_send.at[g]).wait()
        for step in (1, 2, 3):
            along(g, step).wait_send()
    for step in range(4):
        for g in range(3):
            forward(g, step).wait()


def finish(m_ref, z_ref, s_ref, w_ref, n_hbm, p_hbm, q_hbm, nbuf, pbuf, qbuf, sem):
    chunk = 1024
    w = w_ref[...]
    p_t = jnp.dot(w, s_ref[...], precision=HIGH, preferred_element_type=F32)
    pbuf[...] = p_t
    copies = [pltpu.make_async_copy(pbuf, p_hbm, sem.at[0, 2])]
    copies[0].start()
    w_high, w_mid = split(w * (1.0 / 32))
    w_cat = jnp.concatenate([w_high, w_high, w_mid, w_mid], axis=1)
    p_high, p_mid = split(p_t.T)
    p_cat = jnp.concatenate([p_high, p_high, p_mid, p_mid], axis=1)
    for k in range(COLS // chunk):
        @pl.loop(0, chunk // 256)
        def _(i):
            cols = pl.ds(pl.multiple_of(k * chunk + i * 256, 256), 256)
            z_high, z_mid = split(z_ref[:, cols])
            q = jnp.dot(w_cat, jnp.concatenate([z_high, z_mid, z_high, z_mid], axis=0), preferred_element_type=F32)
            qbuf[:, cols] = q
            q_high, q_mid = split(q)
            approx = jnp.dot(p_cat, jnp.concatenate([q_high, q_mid, q_high, q_mid], axis=0), preferred_element_type=F32)
            nbuf[:, cols] = m_ref[:, cols] - approx

        cols = pl.ds(k * chunk, chunk)
        copies.append(pltpu.make_async_copy(nbuf.at[:, cols], n_hbm.at[:, cols], sem.at[k, 0]))
        copies.append(pltpu.make_async_copy(qbuf.at[:, cols], q_hbm.at[:, cols], sem.at[k, 1]))
        copies[-2].start()
        copies[-1].start()
    for copy in copies:
        copy.wait()


def local(grads, errors, q_start):
    vmem = pl.BlockSpec(memory_space=pltpu.VMEM)
    hbm = pl.BlockSpec(memory_space=pl.ANY)
    dma = pltpu.SemaphoreType.DMA
    merged, z_sum, sketch, w = pl.pallas_call(
        exchange,
        out_shape=(pltpu.VMEM((ROWS, COLS), F32), pltpu.VMEM((RANK, COLS), F32), pltpu.VMEM((RANK, ROWS), F32), pltpu.VMEM((RANK, RANK), F32)),
        in_specs=[hbm] * 3,
        out_specs=(vmem,) * 4,
        scratch_shapes=[
            pltpu.VMEM((ROWS, COLS), F32),
            pltpu.VMEM((RANK, COLS), F32),
            pltpu.VMEM((2 * RANK, COLS), BF16),
            pltpu.VMEM((NBLK, 2 * BLK, COLS), BF16),
            pltpu.VMEM((NBLK, RANK, BLK), F32),
            pltpu.VMEM((NBLK, HALF, BLK), F32),
            pltpu.VMEM((NBLK, 16, HALF, BLK), F32),
            pltpu.VMEM((RANK, COLS), F32),
            pltpu.VMEM((4, HALF, SLAB), F32),
            pltpu.VMEM((3, HALF, SLAB), F32),
            pltpu.VMEM((HALF, SLAB), F32),
            pltpu.VMEM((15, HALF, TILE), F32),
            pltpu.VMEM((HALF, TILE), F32),
            pltpu.VMEM((4, RANK, 2 * RANK), F32),
            pltpu.VMEM((NBLK, 2 * RANK, 2 * BLK), BF16),
            dma((4 * NBLK, 3)),
            dma((NBLK,)), dma((NBLK,)), dma((NBLK,)), dma((NBLK,)), dma((NBLK,)), dma((NBLK,)), dma(()), dma(()),
            dma((4,)), dma((4,)), dma((3,)), dma((3,)), dma((3,)), dma((3,)), dma((3,)), dma((3,)), dma((3, 3)), dma((3, 3)),
            dma((3, 4)), dma((3, 4)),
        ],
        compiler_params=pltpu.CompilerParams(collective_id=0, has_side_effects=True, vmem_limit_bytes=36 << 20),
        name="exchange",
    )(grads[0], errors[0], q_start.T)
    new_errors, p_t, q_t = pl.pallas_call(
        finish,
        out_shape=(jax.ShapeDtypeStruct((ROWS, COLS), F32), jax.ShapeDtypeStruct((RANK, ROWS), F32), jax.ShapeDtypeStruct((RANK, COLS), F32)),
        in_specs=[vmem] * 4,
        out_specs=(hbm,) * 3,
        scratch_shapes=[pltpu.VMEM((ROWS, COLS), F32), pltpu.VMEM((RANK, ROWS), F32), pltpu.VMEM((RANK, COLS), F32), dma((8, 3))],
        compiler_params=pltpu.CompilerParams(vmem_limit_bytes=24 << 20),
        name="finish",
    )(merged, z_sum, sketch, w)
    return new_errors[None], p_t.T, q_t.T


def solution(mesh):
    return jax.shard_map(
        local,
        mesh=mesh,
        in_specs=(P("dp", "tensor", None), P("dp", "tensor", None), P()),
        out_specs=(P("dp", "tensor", None), P("tensor", None), P()),
        check_vma=False,
    )
```

time: 335 us -> 74.7 us (0.22)
  waiting for transfers between devices: 250 us -> 0 us
  Pallas kernels: 0 us -> 72.3 us
  matrix products: 40.7 us -> 0 us
  between operations: 14.8 us -> 0.65 us
  blocking collectives: 13.3 us -> 0 us
  other arithmetic: 12.7 us -> 0 us
    psum x2 -> x0, waiting for transfers between devices: 250 us -> none  [the longest x1 151 us: local(): lax.psum(jnp.dot(merged.T, p_orth, precision=high) / replicas, ('dp', 'te...]
    pallas_call x0 -> x2, Pallas kernels: none -> 72.3 us  [the longest x1 59 us: local(): pl.pallas_call(exchange, out_shape=(pltpu.VMEM((ROWS, COLS), F32), pltpu....]
    dot_general x4 -> x0, matrix products: 39.6 us -> none  [the longest x1 13.8 us: local(): approx = jnp.dot(p_orth, q_new.T, precision=high)]
    psum x1 -> x0, blocking collectives: 13.3 us -> none  [local(): gram = lax.psum(jnp.dot(sketch.T, sketch, precision=high), 'tensor')]
    another operation x5 -> x0, other arithmetic: 12.1 us -> none  [the longest x3 6.52 us: local(): lower = jnp.linalg.cholesky(gram)]
  transfers between devices with their start and end apart: 2 -> 0, of which waited for: 2 -> 0; matrix products, arithmetic and copies ran while one was open for 0% -> 0% of each run, Pallas kernels for 0% -> 0%
where the time goes in v1:
time: 74.7 us; the launch traced here: 74.5 us
  Pallas kernels  72.3 us (97%)
  local copies, waits for them, and re-layouts  1.58 us (2%)
    pallas_call x1, Pallas kernels, local(): pl.pallas_call(exchange, out_shape=(pltpu.VMEM((ROWS, COLS), F32), pltpu....  59 us
    pallas_call x1, Pallas kernels, local(): pl.pallas_call(finish, out_shape=(jax.ShapeDtypeStruct((ROWS, COLS), F32)...  13.3 us
    unnamed x2, local copies, waits for them, and re-layouts  1.58 us

profile of v1, /device:TPU:1, one launch (start us, length us, event | category | flops | bytes accessed | tf_op | source)
XLA Modules:
  0.0 74.5 jit_solution(14599753088406666902)
XLA Ops:
  0.6 0.0 copy-start
  0.6 1.6 %copy-done = f32[8192,64]{0,1:T(8,128)S(1)} copy-done((f32[8192,64]{0,1:T(8,128)S(1)}, f32[8192,64]{0,1:T(8,128)}, u32[]{:S(2)}) %copy-start) | copy-done | bytes 2097176
  2.2 59.0 %exchange.1 = (f32[256,8192]{1,0:T(8,128)S(1)}, f32[64,8192]{1,0:T(8,128)S(1)}, f32[64,256]{1,0:T(8,128)S(1)}, f32[64,64]{1,0:T(8,128)S(1)}) custom-call(f32[256,8192]{1,0:T(8,128)} %bitcast.7, f32[256,8192]{1,0:T(8,128)} %bitcast.8, f32[64,8192]{1,0:T(8,128)S(1)} %bitcast.6), custom_call_target="tpu_custom_call" | custom-call | tf_op jit(solution)/shard_map/exchange/pallas_call | solution.py:320
  61.2 13.3 %finish.1 = (f32[256,8192]{1,0:T(8,128)}, f32[64,256]{1,0:T(8,128)}, f32[64,8192]{1,0:T(8,128)}) custom-call(f32[256,8192]{1,0:T(8,128)S(1)} %get-tuple-element.10.m_ref, f32[64,8192]{1,0:T(8,128)S(1)} %get-tuple-element.11.z_ref, f32[64,256]{1,0:T(8,128)S(1)} %get-tuple-element.12.s_ref, f32[64,64]{1,0:T(8,128)S(1)} %get-tuple-element.13.w_ref), custom_call_target="tpu_custom_call" | custom-call | tf_op jit(solution)/shard_map/finish/pallas_call | solution.py:349
Async XLA Ops:
  0.6 1.6 %copy-start = (f32[8192,64]{0,1:T(8,128)S(1)}, f32[8192,64]{0,1:T(8,128)}, u32[]{:S(2)}) copy-start(f32[8192,64]{0,1:T(8,128)} %param.5) | copy-start | bytes 6291460

commit v2 on v0

v2 whole, which is shorter than its diff:
```python
import jax
import jax.numpy as jnp
from jax import lax
from jax.experimental import pallas as pl
from jax.experimental.pallas import tpu as pltpu
from jax.sharding import PartitionSpec as P

MESH = pl.DeviceIdType.MESH
F32, BF16 = jnp.float32, jnp.bfloat16
HIGH = lax.Precision.HIGHEST
ROWS, COLS, RANK, HALF = 256, 8192, 64, 32
BLK = 128
NBLK = ROWS // BLK
CHUNKS = ((1024,) * 8, (1024,) * 7 + (512, 256, 256))
OWN = COLS // 2
SLAB = OWN // 4
STRIP = SLAB // 4
TILE = 128
GROUPS = range(4)
GROUP = 16
PIECES = (512,) * 16
AROUND = [(a, b, c) for a in range(4) for b in range(4) for c in range(4) if (a, b, c) != (0, 0, 0) and 0 in (a, b, c)]


def split(value):
    high = value.astype(BF16)
    return high, (value - high.astype(F32)).astype(BF16)


def mod4(value):
    return lax.rem(value, 4)


def device(x, y, z, c):
    return ((y * 4 + z) * 2 + c, x)


def dot_nt(a, b, precision=None):
    return lax.dot_general(a, b, (((1,), (1,)), ((), ())), precision=precision, preferred_element_type=F32)


def exchange(g_hbm, e_hbm, q_hbm, m_ref, z_ref, p_ref, pcat_ref, wcat_ref,
             ebuf, qbuf, qs, hm, mrx, hm2, spart, sprx, srx, s_ref, lhs, zbuf, rx1, ph2, rx2, gsl,
             in_sem, m_send, m_recv, p_send, p_recv, s_send, s_recv, sp_send, sp_recv, g_send, g_recv,
             r1_send, r1_recv, r2_send, r2_recv, a1_send, a1_recv, a2_send, a2_recv, f_send, f_recv):
    d = lax.axis_index("dp")
    x = lax.axis_index("tensor")
    y, z, c = lax.div(d, 8), mod4(lax.div(d, 2)), lax.rem(d, 2)
    me = y * 4 + z
    partner = device(x, y, z, 1 - c)
    mine = pl.multiple_of(c * HALF, HALF)
    other = pl.multiple_of((1 - c) * HALF, HALF)
    own = pl.multiple_of(c * OWN, OWN)
    theirs = pl.multiple_of((1 - c) * OWN, OWN)

    def remote(src, dst, send, recv, target):
        return pltpu.make_async_remote_copy(src_ref=src, dst_ref=dst, send_sem=send, recv_sem=recv, device_id=target, device_id_type=MESH)

    def all_of(ref, sem):
        pltpu.make_async_copy(ref, ref, sem).wait()

    loads = {}
    for b in range(NBLK):
        begin = 0
        for k, size in enumerate(CHUNKS[b]):
            rows, cols = pl.ds(b * BLK, BLK), pl.ds(begin, size)
            sems = in_sem.at[b * len(CHUNKS[0]) + k]
            parts = [
                pltpu.make_async_copy(g_hbm.at[rows, cols], m_ref.at[rows, cols], sems.at[0]),
                pltpu.make_async_copy(e_hbm.at[rows, cols], ebuf.at[rows, cols], sems.at[1]),
            ]
            if b == 0:
                parts.append(pltpu.make_async_copy(q_hbm.at[:, cols], qbuf.at[:, cols], sems.at[2]))
            for part in parts:
                part.start()
            loads[b, k] = begin, size, parts
            begin += size

    barrier = pltpu.get_barrier_semaphore()
    pl.semaphore_signal(barrier, inc=1, device_id=partner, device_id_type=MESH)
    for dx, dy, dz in AROUND:
        pl.semaphore_signal(barrier, inc=1, device_id=device(mod4(x + dx), mod4(y + dy), mod4(z + dz), c), device_id_type=MESH)

    def left_chunk(b, k):
        begin, size, parts = loads[b, k]
        for part in parts:
            part.wait()
        rows = slice(b * BLK, (b + 1) * BLK)
        for i in range(0, size, 256):
            cols = slice(begin + i, begin + i + 256)
            if b == 0:
                qs[0:RANK, cols], qs[RANK:, cols] = split(qbuf[:, cols])
            merged = m_ref[rows, cols] + ebuf[rows, cols]
            m_ref[rows, cols] = merged
            hm[k % 2, 0:BLK, i:i + 256], hm[k % 2, BLK:, i:i + 256] = split(merged)
        return dot_nt(qs[:, begin:begin + size], hm[k % 2, :, :size])

    def pair_copy(b):
        return remote(spart.at[b, pl.ds(other, HALF)], sprx.at[b], p_send.at[b], p_recv.at[b], partner)

    def merged_copy(b):
        rows = pl.ds(b * BLK, BLK)
        return remote(m_ref.at[rows, pl.ds(theirs, OWN)], mrx.at[rows], m_send.at[b], m_recv.at[b], partner)

    def left_send(b):
        pair_copy(b).wait()
        srx[b, me] = spart[b, pl.ds(mine, HALF)] + sprx[b]

        @pl.loop(1, 16)
        def _(r):
            target = device(x, mod4(y + lax.div(r, 4)), mod4(z + mod4(r)), c)
            remote(srx.at[b, me], srx.at[b, me], s_send.at[b], s_recv.at[b], target).start()

    for b in range(NBLK):
        total = jnp.zeros((2 * RANK, 2 * BLK), F32)
        for k in range(len(CHUNKS[b])):
            total = total + left_chunk(b, k)
            if b > 0 and k == 1:
                left_send(b - 1)
        total = total[:RANK] + total[RANK:]
        spart[b] = total[:, :BLK] + total[:, BLK:]
        if b == 0:
            pl.semaphore_wait(barrier, 1 + len(AROUND))
        pair_copy(b).start()
        merged_copy(b).start()
    left_send(NBLK - 1)

    def left_sum(b):
        fifteen = srx.at[b, pl.ds(0, 15)]
        all_of(fifteen, s_recv.at[b])
        total = srx[b, 0]
        for r in range(1, 16):
            total = total + srx[b, r]
        place = (pl.ds(mine, HALF), pl.ds(b * BLK, BLK))
        s_ref[pl.ds(mine, HALF), b * BLK:(b + 1) * BLK] = total * (1.0 / 32)
        copy = remote(s_ref.at[place], s_ref.at[place], sp_send.at[b], sp_recv.at[b], partner)
        copy.start()
        return copy

    def chip_sum(b):
        merged_copy(b).wait()

        @pl.loop(0, OWN // 256, unroll=4)
        def _(i):
            here = pl.ds(pl.multiple_of(i * 256, 256), 256)
            there = pl.ds(pl.multiple_of(own + i * 256, 256), 256)
            rows = slice(b * BLK, (b + 1) * BLK)
            hm2[b, 0:BLK, here], hm2[b, BLK:, here] = split(m_ref[rows, there] + mrx[rows, here])

    def left_ready(b, copy):
        copy.wait()
        high, mid = split(s_ref[:, b * BLK:(b + 1) * BLK])
        both = jnp.concatenate([high, mid], axis=0)
        lhs[b] = jnp.concatenate([both, both], axis=1)

    def right_part(b, cols):
        total = jnp.dot(lhs[b], hm2[b, :, cols], preferred_element_type=F32)
        return total[:RANK] + total[RANK:]

    copy = left_sum(0)
    chip_sum(0)
    left_ready(0, copy)
    for i in range(0, OWN, 512):
        zbuf[:, i:i + 512] = right_part(0, slice(i, i + 512))
    chip_sum(1)
    copy = left_sum(1)
    left_ready(1, copy)

    def by_turn(g, options):
        if g < 3:
            return options[g]
        return jnp.where(c == 0, options[0], options[1])

    first = [by_turn(g, (x, y, z)) for g in GROUPS]
    second = [by_turn(g, (y, z, x)) for g in GROUPS]
    third = [by_turn(g, (z, x, y)) for g in GROUPS]

    def moved(g, da, db, dc):
        dx, dy, dz = by_turn(g, (da, dc, db)), by_turn(g, (db, da, dc)), by_turn(g, (dc, db, da))
        return device(mod4(x + dx), mod4(y + dy), mod4(z + dz), c)

    def group_rows(g):
        return pl.ds(g * GROUP, GROUP)

    for i in range(0, OWN, 512):
        zbuf[:, i:i + 512] += right_part(1, slice(i, i + 512))

    for step in (2, 1, 3):
        for g in GROUPS:
            k = mod4(first[g] + step)
            src = zbuf.at[group_rows(g), pl.ds(pl.multiple_of(k * SLAB, SLAB), SLAB)]
            remote(src, rx1.at[step - 1, group_rows(g)], r1_send.at[g], r1_recv.at[g], moved(g, step, 0, 0)).start()

    sketch = s_ref[...]
    gsl[x] = jnp.concatenate([dot_nt(sketch, sketch, HIGH), jnp.zeros((RANK, RANK), F32)], axis=1)
    for k in range(3):
        remote(gsl.at[x], gsl.at[x], g_send, g_recv, device(mod4(x + k + 1), y, z, c)).start()

    def tile_of(v, w):
        return pl.ds(pl.multiple_of(lax.rem(w, 2) * 8, 8), 8), pl.multiple_of((v * 2 + lax.div(w, 2)) * TILE, TILE)

    for g in GROUPS:
        all_of(rx1.at[pl.ds(0, 3), group_rows(g)], r1_recv.at[g])
        cols = pl.ds(pl.multiple_of(first[g] * SLAB, SLAB), SLAB)
        rows = slice(g * GROUP, (g + 1) * GROUP)
        ph2[g] = (zbuf[rows, cols] + rx1[0, rows]) + (rx1[1, rows] + rx1[2, rows])

        @pl.loop(1, 16)
        def _(r):
            db, dc = lax.div(r, 4), mod4(r)
            rows, col = tile_of(mod4(second[g] + db), mod4(third[g] + dc))
            remote(ph2.at[g, rows, pl.ds(col, TILE)], rx2.at[g, r - 1], r2_send.at[g], r2_recv.at[g], moved(g, 0, db, dc)).start()

    three = gsl.at[pl.ds(0, 3)]
    all_of(three, g_recv)
    gram = (gsl[0] + gsl[1]) + (gsl[2] + gsl[3])
    lane = lax.broadcasted_iota(jnp.int32, (RANK, 2 * RANK), 1)
    sub = lax.broadcasted_iota(jnp.int32, (RANK, 2 * RANK), 0)
    diagonal = jnp.where(lane == sub, gram, 0.0)
    trace = jnp.sum(jnp.sum(diagonal, axis=1, keepdims=True), axis=0, keepdims=True)
    mat = gram + jnp.where(lane == sub, 1e-05 * (trace / RANK), 0.0) + jnp.where(lane == sub + RANK, 1.0, 0.0)
    row_id = lax.broadcasted_iota(jnp.int32, (RANK, 1), 0)

    def eliminate(mat, begin, end):
        for j in range(begin, end):
            pivot = mat[j:j + 1, :]
            factor = jnp.where(row_id > j, mat[:, j:j + 1] / mat[j:j + 1, j:j + 1], 0.0)
            mat = mat - factor * pivot
        return mat

    mat = eliminate(mat, 0, RANK // 2)

    for g in GROUPS:
        all_of(rx2.at[g], r2_recv.at[g])
        rows, col = tile_of(second[g], third[g])
        total = ph2[g, rows, pl.ds(col, TILE)]
        for r in range(15):
            total = total + rx2[g, r]
        rows = pl.ds(pl.multiple_of(g * GROUP + lax.rem(third[g], 2) * 8, 8), 8)
        place = (rows, pl.ds(pl.multiple_of(own + first[g] * SLAB + col, TILE), TILE))
        z_ref[place] = total

        @pl.loop(1, 16)
        def _(r):
            remote(z_ref.at[place], z_ref.at[place], a1_send.at[g], a1_recv.at[g, lax.div(r, 4)], moved(g, 0, lax.div(r, 4), mod4(r))).start()

    mat = eliminate(mat, RANK // 2, RANK)
    scale = jnp.sum(jnp.where(lane == sub, mat, 0.0), axis=1, keepdims=True)
    inverse = mat[:, RANK:] / jnp.sqrt(scale)
    parts = jnp.concatenate(split(inverse * (1.0 / 32)), axis=0)
    wcat_ref[...] = jnp.concatenate([parts, parts], axis=1)

    def slab(g, v):
        return z_ref.at[group_rows(g), pl.ds(pl.multiple_of(own + v * SLAB, SLAB), SLAB)]

    def forward(g, step):
        here = slab(g, mod4(first[g] + step))
        return remote(here, here, f_send.at[g, step], f_recv.at[g, step], partner)

    def along(g, step, away):
        cols = pl.ds(pl.multiple_of(own + first[g] * SLAB + mod4(second[g] + 4 - away) * STRIP, STRIP), STRIP)
        here = z_ref.at[group_rows(g), cols]
        return remote(here, here, a2_send.at[g, step - 1], a2_recv.at[g, step - 1], moved(g, step, 0, 0))

    fifteen = [z_ref.at[pl.ds(g * GROUP, 8), pl.ds(0, 15 * TILE)] for g in GROUPS]
    for away in (0, 1, 3, 2):
        for g in GROUPS:
            all_of(z_ref.at[pl.ds(g * GROUP, 8), pl.ds(0, (4 if away else 3) * TILE)], a1_recv.at[g, away])
            for step in (2, 1, 3):
                along(g, step, away).start()
    for g in GROUPS:
        forward(g, 0).start()
    p_t = jnp.dot(inverse, sketch, precision=HIGH, preferred_element_type=F32)
    p_ref[...] = p_t
    high, mid = split(p_t.T)
    pcat_ref[...] = jnp.concatenate([high, high, mid], axis=1)
    for step in (1, 3, 2):
        for g in GROUPS:
            all_of(slab(g, 0), a2_recv.at[g, step - 1])
            forward(g, 4 - step).start()

    for b in range(NBLK):
        all_of(srx.at[b, pl.ds(0, 15)], s_send.at[b])
    all_of(three, g_send)
    for g in GROUPS:
        all_of(rx1.at[pl.ds(0, 3), group_rows(g)], r1_send.at[g])
        all_of(rx2.at[g], r2_send.at[g])
        all_of(fifteen[g], a1_send.at[g])
        for step in (1, 2, 3):
            all_of(slab(g, 0), a2_send.at[g, step - 1])
    for step in range(4):
        for g in GROUPS:
            forward(g, step).wait()


def finish(m_ref, z_ref, p_ref, pcat_ref, wcat_ref, n_hbm, p_hbm, q_hbm, nbuf, qbuf, sem):
    copies = []

    def write(k, cols, q3):
        nbuf[:, cols] = m_ref[:, cols] - jnp.dot(pcat_ref[...], q3, preferred_element_type=F32)
        copies.append(pltpu.make_async_copy(nbuf.at[:, cols], n_hbm.at[:, cols], sem.at[k, 0]))
        copies[-1].start()

    begin, last = 0, None
    for k, size in enumerate(PIECES):
        cols = pl.ds(begin, size)
        begin += size
        q = jnp.dot(wcat_ref[...], jnp.concatenate(split(z_ref[:, cols]), axis=0), preferred_element_type=F32)
        q = q[:RANK] + q[RANK:]
        qbuf[:, cols] = q
        high, mid = split(q)
        q3 = jnp.concatenate([high, mid, high], axis=0)
        if last is not None:
            write(*last)
        last = (k, cols, q3)
    copies.append(pltpu.make_async_copy(qbuf, q_hbm, sem.at[0, 1]))
    copies[-1].start()
    write(*last)
    copies.append(pltpu.make_async_copy(p_ref, p_hbm, sem.at[0, 2]))
    copies[-1].start()
    for copy in copies:
        copy.wait()


def local(grads, errors, q_start):
    vmem = pl.BlockSpec(memory_space=pltpu.VMEM)
    hbm = pl.BlockSpec(memory_space=pl.ANY)
    dma = pltpu.SemaphoreType.DMA
    parts = pl.pallas_call(
        exchange,
        out_shape=(
            pltpu.VMEM((ROWS, COLS), F32), pltpu.VMEM((RANK, COLS), F32), pltpu.VMEM((RANK, ROWS), F32),
            pltpu.VMEM((ROWS, 3 * RANK), BF16), pltpu.VMEM((2 * RANK, 2 * RANK), BF16),
        ),
        in_specs=[hbm] * 3,
        out_specs=(vmem,) * 5,
        scratch_shapes=[
            pltpu.VMEM((ROWS, COLS), F32),
            pltpu.VMEM((RANK, COLS), F32),
            pltpu.VMEM((2 * RANK, COLS), BF16),
            pltpu.VMEM((2, 2 * BLK, max(CHUNKS[0])), BF16),
            pltpu.VMEM((ROWS, OWN), F32),
            pltpu.VMEM((NBLK, 2 * BLK, OWN), BF16),
            pltpu.VMEM((NBLK, RANK, BLK), F32),
            pltpu.VMEM((NBLK, HALF, BLK), F32),
            pltpu.VMEM((NBLK, 16, HALF, BLK), F32),
            pltpu.VMEM((RANK, ROWS), F32),
            pltpu.VMEM((NBLK, 2 * RANK, 2 * BLK), BF16),
            pltpu.VMEM((RANK, OWN), F32),
            pltpu.VMEM((3, RANK, SLAB), F32),
            pltpu.VMEM((4, GROUP, SLAB), F32),
            pltpu.VMEM((4, 15, 8, TILE), F32),
            pltpu.VMEM((4, RANK, 2 * RANK), F32),
            dma((sum(map(len, CHUNKS)), 3)),
            dma((NBLK,)), dma((NBLK,)), dma((NBLK,)), dma((NBLK,)), dma((NBLK,)), dma((NBLK,)), dma((NBLK,)), dma((NBLK,)), dma(()), dma(()),
            dma((4,)), dma((4,)), dma((4,)), dma((4,)), dma((4,)), dma((4, 4)), dma((4, 3)), dma((4, 3)), dma((4, 4)), dma((4, 4)),
        ],
        compiler_params=pltpu.CompilerParams(collective_id=0, has_side_effects=True, vmem_limit_bytes=52 << 20),
        name="exchange",
    )(grads[0], errors[0], q_start.T)
    new_errors, p_t, q_t = pl.pallas_call(
        finish,
        out_shape=(jax.ShapeDtypeStruct((ROWS, COLS), F32), jax.ShapeDtypeStruct((RANK, ROWS), F32), jax.ShapeDtypeStruct((RANK, COLS), F32)),
        in_specs=[vmem] * 5,
        out_specs=(hbm,) * 3,
        scratch_shapes=[pltpu.VMEM((ROWS, COLS), F32), pltpu.VMEM((RANK, COLS), F32), dma((len(PIECES), 3))],
        compiler_params=pltpu.CompilerParams(vmem_limit_bytes=24 << 20),
        name="finish",
    )(*parts)
    return new_errors[None], p_t.T, q_t.T


def solution(mesh):
    return jax.shard_map(
        local,
        mesh=mesh,
        in_specs=(P("dp", "tensor", None), P("dp", "tensor", None), P()),
        out_specs=(P("dp", "tensor", None), P("tensor", None), P()),
        check_vma=False,
    )
```

time: 335 us -> 53.5 us (0.16)
  waiting for transfers between devices: 250 us -> 0 us
  Pallas kernels: 0 us -> 52.7 us
  matrix products: 40.7 us -> 0 us
  between operations: 14.8 us -> 0.64 us
  blocking collectives: 13.3 us -> 0 us
  other arithmetic: 12.7 us -> 0 us
    psum x2 -> x0, waiting for transfers between devices: 250 us -> none  [the longest x1 151 us: local(): lax.psum(jnp.dot(merged.T, p_orth, precision=high) / replicas, ('dp', 'te...]
    pallas_call x0 -> x2, Pallas kernels: none -> 52.7 us  [the longest x1 48 us: local(): pl.pallas_call(exchange, out_shape=(pltpu.VMEM((ROWS, COLS), F32), pltpu....]
    dot_general x4 -> x0, matrix products: 39.6 us -> none  [the longest x1 13.8 us: local(): approx = jnp.dot(p_orth, q_new.T, precision=high)]
    psum x1 -> x0, blocking collectives: 13.3 us -> none  [local(): gram = lax.psum(jnp.dot(sketch.T, sketch, precision=high), 'tensor')]
    another operation x5 -> x0, other arithmetic: 12.1 us -> none  [the longest x3 6.52 us: local(): lower = jnp.linalg.cholesky(gram)]
  transfers between devices with their start and end apart: 2 -> 0, of which waited for: 2 -> 0; matrix products, arithmetic and copies ran while one was open for 0% -> 0% of each run, Pallas kernels for 0% -> 0%
where the time goes in v2:
time: 53.5 us; the launch traced here: 53.4 us
  Pallas kernels  52.7 us (99%)
  between operations  0.64 us (1%)
    pallas_call x1, Pallas kernels, local(): pl.pallas_call(exchange, out_shape=(pltpu.VMEM((ROWS, COLS), F32), pltpu....  48 us
    pallas_call x1, Pallas kernels, local(): pl.pallas_call(finish, out_shape=(jax.ShapeDtypeStruct((ROWS, COLS), F32)...  4.74 us

profile of v2, /device:TPU:1, one launch (start us, length us, event | category | flops | bytes accessed | tf_op | source)
XLA Modules:
  0.0 53.4 jit_solution(18367134343305775736)
XLA Ops:
  0.6 48.0 %exchange.1 = (f32[256,8192]{1,0:T(8,128)S(1)}, f32[64,8192]{1,0:T(8,128)S(1)}, f32[64,256]{1,0:T(8,128)S(1)}, bf16[256,192]{1,0:T(8,128)(2,1)S(1)}, bf16[128,128]{1,0:T(8,128)(2,1)S(1)}) custom-call(f32[256,8192]{1,0:T(8,128)} %bitcast.6, f32[256,8192]{1,0:T(8,128)} %bitcast.7, f32[64,8192]{1,0:T(8,128)} %bitcast.8), custom_call_target="tpu_custom_call" | custom-call | tf_op jit(solution)/shard_map/exchange/pallas_call | solution.py:329
  48.6 4.7 %finish.1 = (f32[256,8192]{1,0:T(8,128)}, f32[64,256]{1,0:T(8,128)}, f32[64,8192]{1,0:T(8,128)}) custom-call(f32[256,8192]{1,0:T(8,128)S(1)} %get-tuple-element.11.m_ref, f32[64,8192]{1,0:T(8,128)S(1)} %get-tuple-element.12.z_ref, f32[64,256]{1,0:T(8,128)S(1)} %get-tuple-element.13.p_ref, bf16[256,192]{1,0:T(8,128)(2,1)S(1)} %get-tuple-element.14.pcat_ref, ...), custom_call_target="tpu_custom_call" | custom-call | tf_op jit(solution)/shard_map/finish/pallas_call | solution.py:361

commit v3 on v2

--- a/solution.py
+++ b/solution.py
@@ -16,7 +16,7 @@
 SLAB = OWN // 4
 STRIP = SLAB // 4
 TILE = 128
-GROUPS = range(4)
+GROUPS = 4
 GROUP = 16
 PIECES = (512,) * 16
 AROUND = [(a, b, c) for a in range(4) for b in range(4) for c in range(4) if (a, b, c) != (0, 0, 0) and 0 in (a, b, c)]
@@ -28,7 +28,7 @@
 
 
 def mod4(value):
-    return lax.rem(value, 4)
+    return jnp.where(value > 3, value - 4, value)
 
 
 def device(x, y, z, c):
@@ -40,12 +40,12 @@
 
 
 def exchange(g_hbm, e_hbm, q_hbm, m_ref, z_ref, p_ref, pcat_ref, wcat_ref,
-             ebuf, qbuf, qs, hm, mrx, hm2, spart, sprx, srx, s_ref, lhs, zbuf, rx1, ph2, rx2, gsl,
+             ebuf, qbuf, qs, hm, mrx, hm2, spart, sprx, srx, s_ref, zbuf, rx1, ph2, rx2, gsl,
              in_sem, m_send, m_recv, p_send, p_recv, s_send, s_recv, sp_send, sp_recv, g_send, g_recv,
              r1_send, r1_recv, r2_send, r2_recv, a1_send, a1_recv, a2_send, a2_recv, f_send, f_recv):
     d = lax.axis_index("dp")
     x = lax.axis_index("tensor")
-    y, z, c = lax.div(d, 8), mod4(lax.div(d, 2)), lax.rem(d, 2)
+    y, z, c = lax.div(d, 8), lax.rem(lax.div(d, 2), 4), lax.rem(d, 2)
     me = y * 4 + z
     partner = device(x, y, z, 1 - c)
     mine = pl.multiple_of(c * HALF, HALF)
@@ -108,7 +108,7 @@
 
         @pl.loop(1, 16)
         def _(r):
-            target = device(x, mod4(y + lax.div(r, 4)), mod4(z + mod4(r)), c)
+            target = device(x, mod4(y + lax.div(r, 4)), mod4(z + lax.rem(r, 4)), c)
             remote(srx.at[b, me], srx.at[b, me], s_send.at[b], s_recv.at[b], target).start()
 
     for b in range(NBLK):
@@ -135,7 +135,7 @@
         s_ref[pl.ds(mine, HALF), b * BLK:(b + 1) * BLK] = total * (1.0 / 32)
         copy = remote(s_ref.at[place], s_ref.at[place], sp_send.at[b], sp_recv.at[b], partner)
         copy.start()
-        return copy
+        return copy, total * (1.0 / 32)
 
     def chip_sum(b):
         merged_copy(b).wait()
@@ -149,47 +149,52 @@
 
     def left_ready(b, copy):
         copy.wait()
-        high, mid = split(s_ref[:, b * BLK:(b + 1) * BLK])
-        both = jnp.concatenate([high, mid], axis=0)
-        lhs[b] = jnp.concatenate([both, both], axis=1)
-
-    def right_part(b, cols):
-        total = jnp.dot(lhs[b], hm2[b, :, cols], preferred_element_type=F32)
-        return total[:RANK] + total[RANK:]
-
-    copy = left_sum(0)
+        return s_ref[:, b * BLK:(b + 1) * BLK]
+
+    def right_part(b, left, cols):
+        both = jnp.concatenate(split(left), axis=0)
+        total = jnp.dot(jnp.concatenate([both, both], axis=1), hm2[b, :, cols], preferred_element_type=F32)
+        return total[:left.shape[0]] + total[left.shape[0]:]
+
+    copy, _ = left_sum(0)
     chip_sum(0)
-    left_ready(0, copy)
+    left = left_ready(0, copy)
     for i in range(0, OWN, 512):
-        zbuf[:, i:i + 512] = right_part(0, slice(i, i + 512))
+        zbuf[:, i:i + 512] = right_part(0, left, slice(i, i + 512))
     chip_sum(1)
-    copy = left_sum(1)
-    left_ready(1, copy)
-
-    def by_turn(g, options):
-        if g < 3:
-            return options[g]
-        return jnp.where(c == 0, options[0], options[1])
-
-    first = [by_turn(g, (x, y, z)) for g in GROUPS]
-    second = [by_turn(g, (y, z, x)) for g in GROUPS]
-    third = [by_turn(g, (z, x, y)) for g in GROUPS]
+    copy, left = left_sum(1)
+
+    def turned(g):
+        axis = jnp.where(c == 0, jnp.where(g > 2, 0, g), jnp.where(g > 2, 1, 2 - g))
+        return lambda a, b, c: jnp.where(axis == 0, a, jnp.where(axis == 1, b, c))
+
+    def placed(g):
+        pick = turned(g)
+        return pick(x, y, z), pick(y, z, x), pick(z, x, y)
 
     def moved(g, da, db, dc):
-        dx, dy, dz = by_turn(g, (da, dc, db)), by_turn(g, (db, da, dc)), by_turn(g, (dc, db, da))
+        pick = turned(g)
+        dx, dy, dz = pick(da, dc, db), pick(db, da, dc), pick(dc, db, da)
         return device(mod4(x + dx), mod4(y + dy), mod4(z + dz), c)
 
-    def group_rows(g):
-        return pl.ds(g * GROUP, GROUP)
-
-    for i in range(0, OWN, 512):
-        zbuf[:, i:i + 512] += right_part(1, slice(i, i + 512))
-
-    for step in (2, 1, 3):
-        for g in GROUPS:
-            k = mod4(first[g] + step)
+    def group_rows(g, row=0, rows=GROUP):
+        return pl.ds(pl.multiple_of(mod4(2 * c + g) * GROUP + row, rows), rows)
+
+    for half in range(2):
+        if half:
+            copy.wait()
+            left = s_ref[pl.ds(other, HALF), BLK:]
+        ranks = pl.ds(other if half else mine, HALF)
+        for i in range(0, OWN, 512):
+            zbuf[ranks, i:i + 512] += right_part(1, left, slice(i, i + 512))
+
+        @pl.loop(0, 6)
+        def _(i):
+            step = jnp.where(i < 2, 2, jnp.where(i < 4, 1, 3))
+            g = 2 * half + lax.rem(i, 2)
+            k = mod4(placed(g)[0] + step)
             src = zbuf.at[group_rows(g), pl.ds(pl.multiple_of(k * SLAB, SLAB), SLAB)]
-            remote(src, rx1.at[step - 1, group_rows(g)], r1_send.at[g], r1_recv.at[g], moved(g, step, 0, 0)).start()
+            remote(src, rx1.at[g, step - 1], r1_send.at[g], r1_recv.at[g], moved(g, step, 0, 0)).start()
 
     sketch = s_ref[...]
     gsl[x] = jnp.concatenate([dot_nt(sketch, sketch, HIGH), jnp.zeros((RANK, RANK), F32)], axis=1)
@@ -199,16 +204,17 @@
     def tile_of(v, w):
         return pl.ds(pl.multiple_of(lax.rem(w, 2) * 8, 8), 8), pl.multiple_of((v * 2 + lax.div(w, 2)) * TILE, TILE)
 
-    for g in GROUPS:
-        all_of(rx1.at[pl.ds(0, 3), group_rows(g)], r1_recv.at[g])
-        cols = pl.ds(pl.multiple_of(first[g] * SLAB, SLAB), SLAB)
-        rows = slice(g * GROUP, (g + 1) * GROUP)
-        ph2[g] = (zbuf[rows, cols] + rx1[0, rows]) + (rx1[1, rows] + rx1[2, rows])
+    @pl.loop(0, GROUPS)
+    def _(g):
+        first, second, third = placed(g)
+        all_of(rx1.at[g], r1_recv.at[g])
+        cols = pl.ds(pl.multiple_of(first * SLAB, SLAB), SLAB)
+        ph2[g] = (zbuf[group_rows(g), cols] + rx1[g, 0]) + (rx1[g, 1] + rx1[g, 2])
 
         @pl.loop(1, 16)
         def _(r):
-            db, dc = lax.div(r, 4), mod4(r)
-            rows, col = tile_of(mod4(second[g] + db), mod4(third[g] + dc))
+            db, dc = lax.div(r, 4), lax.rem(r, 4)
+            rows, col = tile_of(mod4(second + db), mod4(third + dc))
             remote(ph2.at[g, rows, pl.ds(col, TILE)], rx2.at[g, r - 1], r2_send.at[g], r2_recv.at[g], moved(g, 0, db, dc)).start()
 
     three = gsl.at[pl.ds(0, 3)]
@@ -230,19 +236,22 @@
 
     mat = eliminate(mat, 0, RANK // 2)
 
-    for g in GROUPS:
+    @pl.loop(0, GROUPS)
+    def _(g):
+        first, second, third = placed(g)
         all_of(rx2.at[g], r2_recv.at[g])
-        rows, col = tile_of(second[g], third[g])
+        rows, col = tile_of(second, third)
         total = ph2[g, rows, pl.ds(col, TILE)]
         for r in range(15):
             total = total + rx2[g, r]
-        rows = pl.ds(pl.multiple_of(g * GROUP + lax.rem(third[g], 2) * 8, 8), 8)
-        place = (rows, pl.ds(pl.multiple_of(own + first[g] * SLAB + col, TILE), TILE))
+        rows = group_rows(g, lax.rem(third, 2) * 8, 8)
+        place = (rows, pl.ds(pl.multiple_of(own + first * SLAB + col, TILE), TILE))
         z_ref[place] = total
 
         @pl.loop(1, 16)
         def _(r):
-            remote(z_ref.at[place], z_ref.at[place], a1_send.at[g], a1_recv.at[g, lax.div(r, 4)], moved(g, 0, lax.div(r, 4), mod4(r))).start()
+            db, dc = lax.div(r, 4), lax.rem(r, 4)
+            remote(z_ref.at[place], z_ref.at[place], a1_send.at[g], a1_recv.at[g, db], moved(g, 0, db, dc)).start()
 
     mat = eliminate(mat, RANK // 2, RANK)
     scale = jnp.sum(jnp.where(lane == sub, mat, 0.0), axis=1, keepdims=True)
@@ -254,43 +263,57 @@
         return z_ref.at[group_rows(g), pl.ds(pl.multiple_of(own + v * SLAB, SLAB), SLAB)]
 
     def forward(g, step):
-        here = slab(g, mod4(first[g] + step))
+        here = slab(g, mod4(placed(g)[0] + step))
         return remote(here, here, f_send.at[g, step], f_recv.at[g, step], partner)
 
     def along(g, step, away):
-        cols = pl.ds(pl.multiple_of(own + first[g] * SLAB + mod4(second[g] + 4 - away) * STRIP, STRIP), STRIP)
+        first, second, _ = placed(g)
+        cols = pl.ds(pl.multiple_of(own + first * SLAB + mod4(second + 4 - away) * STRIP, STRIP), STRIP)
         here = z_ref.at[group_rows(g), cols]
         return remote(here, here, a2_send.at[g, step - 1], a2_recv.at[g, step - 1], moved(g, step, 0, 0))
 
-    fifteen = [z_ref.at[pl.ds(g * GROUP, 8), pl.ds(0, 15 * TILE)] for g in GROUPS]
-    for away in (0, 1, 3, 2):
-        for g in GROUPS:
-            all_of(z_ref.at[pl.ds(g * GROUP, 8), pl.ds(0, (4 if away else 3) * TILE)], a1_recv.at[g, away])
-            for step in (2, 1, 3):
-                along(g, step, away).start()
-    for g in GROUPS:
+    def strip_on(g, away, tiles):
+        all_of(z_ref.at[pl.ds(0, 8), pl.ds(0, tiles * TILE)], a1_recv.at[g, away])
+        for step in (2, 1, 3):
+            along(g, step, away).start()
+
+    @pl.loop(0, GROUPS)
+    def _(g):
+        strip_on(g, 0, 3)
+
+    @pl.loop(0, 3 * GROUPS)
+    def _(i):
+        strip_on(lax.rem(i, 4), jnp.where(i < 4, 1, jnp.where(i < 8, 3, 2)), 4)
+
+    @pl.loop(0, GROUPS)
+    def _(g):
         forward(g, 0).start()
+
     p_t = jnp.dot(inverse, sketch, precision=HIGH, preferred_element_type=F32)
     p_ref[...] = p_t
     high, mid = split(p_t.T)
     pcat_ref[...] = jnp.concatenate([high, high, mid], axis=1)
-    for step in (1, 3, 2):
-        for g in GROUPS:
-            all_of(slab(g, 0), a2_recv.at[g, step - 1])
-            forward(g, 4 - step).start()
+    @pl.loop(0, 3 * GROUPS)
+    def _(i):
+        g, step = lax.rem(i, 4), jnp.where(i < 4, 1, jnp.where(i < 8, 3, 2))
+        all_of(slab(g, 0), a2_recv.at[g, step - 1])
+        forward(g, 4 - step).start()
 
     for b in range(NBLK):
         all_of(srx.at[b, pl.ds(0, 15)], s_send.at[b])
     all_of(three, g_send)
-    for g in GROUPS:
-        all_of(rx1.at[pl.ds(0, 3), group_rows(g)], r1_send.at[g])
+
+    @pl.loop(0, GROUPS)
+    def _(g):
+        all_of(rx1.at[g], r1_send.at[g])
         all_of(rx2.at[g], r2_send.at[g])
-        all_of(fifteen[g], a1_send.at[g])
-        for step in (1, 2, 3):
-            all_of(slab(g, 0), a2_send.at[g, step - 1])
-    for step in range(4):
-        for g in GROUPS:
-            forward(g, step).wait()
+        all_of(z_ref.at[pl.ds(0, 8), pl.ds(0, 15 * TILE)], a1_send.at[g])
+        for step in range(3):
+            all_of(slab(g, 0), a2_send.at[g, step])
+
+    @pl.loop(0, 4 * GROUPS)
+    def _(i):
+        forward(lax.rem(i, 4), lax.div(i, 4)).wait()
 
 
 def finish(m_ref, z_ref, p_ref, pcat_ref, wcat_ref, n_hbm, p_hbm, q_hbm, nbuf, qbuf, sem):
@@ -345,9 +368,8 @@
             pltpu.VMEM((NBLK, HALF, BLK), F32),
             pltpu.VMEM((NBLK, 16, HALF, BLK), F32),
             pltpu.VMEM((RANK, ROWS), F32),
-            pltpu.VMEM((NBLK, 2 * RANK, 2 * BLK), BF16),
             pltpu.VMEM((RANK, OWN), F32),
-            pltpu.VMEM((3, RANK, SLAB), F32),
+            pltpu.VMEM((4, 3, GROUP, SLAB), F32),
             pltpu.VMEM((4, GROUP, SLAB), F32),
             pltpu.VMEM((4, 15, 8, TILE), F32),
             pltpu.VMEM((4, RANK, 2 * RANK), F32),

time: 53.5 us -> 52.9 us (0.989)
  Pallas kernels: 52.7 us -> 52.1 us
    pallas_call x1, Pallas kernels: 48 us -> 47.4 us  [local(): pl.pallas_call(exchange, out_shape=(pltpu.VMEM((ROWS, COLS), F32), pltpu....]
where the time goes in v3:
time: 52.9 us; the launch traced here: 52.8 us
  Pallas kernels  52.1 us (98%)
  between operations  0.64 us (1%)
    pallas_call x1, Pallas kernels, local(): pl.pallas_call(exchange, out_shape=(pltpu.VMEM((ROWS, COLS), F32), pltpu....  47.4 us
    pallas_call x1, Pallas kernels, local(): pl.pallas_call(finish, out_shape=(jax.ShapeDtypeStruct((ROWS, COLS), F32)...  4.74 us

profile of v3, /device:TPU:1, one launch (start us, length us, event | category | flops | bytes accessed | tf_op | source)
XLA Modules:
  0.0 52.8 jit_solution(951985912238840135)
XLA Ops:
  0.6 47.4 %exchange.1 = (f32[256,8192]{1,0:T(8,128)S(1)}, f32[64,8192]{1,0:T(8,128)S(1)}, f32[64,256]{1,0:T(8,128)S(1)}, bf16[256,192]{1,0:T(8,128)(2,1)S(1)}, bf16[128,128]{1,0:T(8,128)(2,1)S(1)}) custom-call(f32[256,8192]{1,0:T(8,128)} %bitcast.6, f32[256,8192]{1,0:T(8,128)} %bitcast.7, f32[64,8192]{1,0:T(8,128)} %bitcast.8), custom_call_target="tpu_custom_call" | custom-call | tf_op jit(solution)/shard_map/exchange/pallas_call | solution.py:352
  48.0 4.7 %finish.1 = (f32[256,8192]{1,0:T(8,128)}, f32[64,256]{1,0:T(8,128)}, f32[64,8192]{1,0:T(8,128)}) custom-call(f32[256,8192]{1,0:T(8,128)S(1)} %get-tuple-element.11.m_ref, f32[64,8192]{1,0:T(8,128)S(1)} %get-tuple-element.12.z_ref, f32[64,256]{1,0:T(8,128)S(1)} %get-tuple-element.13.p_ref, bf16[256,192]{1,0:T(8,128)(2,1)S(1)} %get-tuple-element.14.pcat_ref, ...), custom_call_target="tpu_custom_call" | custom-call | tf_op jit(solution)/shard_map/finish/pallas_call | solution.py:383

commit v4 on v3

--- a/solution.py
+++ b/solution.py
@@ -190,8 +190,9 @@
 
         @pl.loop(0, 6)
         def _(i):
-            step = jnp.where(i < 2, 2, jnp.where(i < 4, 1, 3))
-            g = 2 * half + lax.rem(i, 2)
+            turn = lax.rem(i, 3)
+            step = jnp.where(turn == 0, 2, jnp.where(turn == 1, 1, 3))
+            g = 2 * half + lax.div(i, 3)
             k = mod4(placed(g)[0] + step)
             src = zbuf.at[group_rows(g), pl.ds(pl.multiple_of(k * SLAB, SLAB), SLAB)]
             remote(src, rx1.at[g, step - 1], r1_send.at[g], r1_recv.at[g], moved(g, step, 0, 0)).start()

time: 52.9 us -> 53 us (level)
  no operation moved by 1% of the time
where the time goes in v4:
time: 53 us; the launch traced here: 52.9 us
  Pallas kernels  52.2 us (98%)
  between operations  0.64 us (1%)
    pallas_call x1, Pallas kernels, local(): pl.pallas_call(exchange, out_shape=(pltpu.VMEM((ROWS, COLS), F32), pltpu....  47.5 us
    pallas_call x1, Pallas kernels, local(): pl.pallas_call(finish, out_shape=(jax.ShapeDtypeStruct((ROWS, COLS), F32)...  4.74 us

profile of v4, /device:TPU:1, one launch (start us, length us, event | category | flops | bytes accessed | tf_op | source)
XLA Modules:
  0.0 52.9 jit_solution(4667975710515091881)
XLA Ops:
  0.6 47.5 %exchange.1 = (f32[256,8192]{1,0:T(8,128)S(1)}, f32[64,8192]{1,0:T(8,128)S(1)}, f32[64,256]{1,0:T(8,128)S(1)}, bf16[256,192]{1,0:T(8,128)(2,1)S(1)}, bf16[128,128]{1,0:T(8,128)(2,1)S(1)}) custom-call(f32[256,8192]{1,0:T(8,128)} %bitcast.6, f32[256,8192]{1,0:T(8,128)} %bitcast.7, f32[64,8192]{1,0:T(8,128)} %bitcast.8), custom_call_target="tpu_custom_call" | custom-call | tf_op jit(solution)/shard_map/exchange/pallas_call | solution.py:353
  48.1 4.7 %finish.1 = (f32[256,8192]{1,0:T(8,128)}, f32[64,256]{1,0:T(8,128)}, f32[64,8192]{1,0:T(8,128)}) custom-call(f32[256,8192]{1,0:T(8,128)S(1)} %get-tuple-element.11.m_ref, f32[64,8192]{1,0:T(8,128)S(1)} %get-tuple-element.12.z_ref, f32[64,256]{1,0:T(8,128)S(1)} %get-tuple-element.13.p_ref, bf16[256,192]{1,0:T(8,128)(2,1)S(1)} %get-tuple-element.14.pcat_ref, ...), custom_call_target="tpu_custom_call" | custom-call | tf_op jit(solution)/shard_map/finish/pallas_call | solution.py:384
